TPU v7x, 32 devices: a whole 2x2x4 slice. The times are simulated.
32 devices in a mesh: seq: 4 (over z), exp: 8 (over y, x, core).
Axes of the slice: x: 2, y: 2, z: 4, core: 2. Of those that a mesh axis runs over, the one named last changes fastest.
Arguments:
- queries: bfloat16 [512, 2048], P('seq', 'exp'), may hold values from -6 to 6
- key_matrix: bfloat16 [512, 2048], P('seq', 'exp'), may hold values from -6 to 6
- values: bfloat16 [512, 2048], P('seq', 'exp'), may hold values from -6 to 6
- log_decay: float32 [16, 512], P('exp', 'seq'), may hold values from -3 to 0
- residual: bfloat16 [512, 3072], P('seq'), may hold values from -6 to 6
- out_weight: bfloat16 [3072, 2048], P('seq', 'exp'), may hold values from -0.125 to 0.125
- router: bfloat16 [3072, 8], replicated, may hold values from -0.109375 to 0.109375
- expert_ids: int32 [512, 2], P('seq'), may hold values from 0 to 7, all different within a row; in each aligned block of 128 rows (0 to 127, 128 to 255, ...) at most 48 rows name the same one
- up_weight: bfloat16 [8, 3072, 4608], P('exp', None, 'seq'), may hold values from -0.109375 to 0.109375
- down_weight: bfloat16 [8, 4608, 3072], P('exp', 'seq'), may hold values from -0.09375 to 0.09375
Outputs:
- layer_out: bfloat16 [512, 3072], P(('seq', 'exp'))
Inputs may be any that keep to these rules, and one draw needn't show every extreme that they name: `expert_ids`: in each aligned block of 128 rows (one sequence block) no expert is named by more than 48 rows, a bound that some block reaches; a row names 2 different experts.
All inputs are finite; a program needn't handle non-finite values.
Results may differ from a plain program's by a relative error of at most 0.015.
Values may be sent and summed in bfloat16 or wider, within the bound.
A program may use at most 64 MiB of HBM per device.

v0:
```python
import jax
import jax.numpy as jnp
from jax import lax
from jax.sharding import PartitionSpec as P


def prefix(x, axis, combine, identity):
    length, index = (lax.axis_size(axis), lax.axis_index(axis))
    everything = jax.tree.map(
        lambda part, kind: lax.all_gather(part.astype(kind), axis), x, (jnp.bfloat16, jnp.bfloat16)
    )
    start = jax.tree.map(
        lambda part, zero: jnp.broadcast_to(jnp.asarray(zero, part.dtype), part.shape), x, identity
    )

    def turn(k, before):
        reached = k < index
        new = combine(
            before, jax.tree.map(lambda part, own: part[k].astype(own.dtype), everything, x)
        )
        return jax.tree.map(lambda a, b: jnp.where(reached, a, b), new, before)

    return lax.fori_loop(0, length, turn, start)


def compose(earlier, later):
    return (earlier[0] * later[0], later[0][:, None, None] * earlier[1] + later[1])


def shards(
    queries,
    key_matrix,
    values,
    log_decay,
    residual,
    out_weight,
    router,
    expert_ids,
    up_weight,
    down_weight,
):
    rows = queries.shape[0]
    heads_here = log_decay.shape[0]
    width = queries.shape[1] // heads_here

    def split_heads(array):
        return array.astype(jnp.float32).reshape(rows, heads_here, width).transpose(1, 0, 2)

    qloc = split_heads(queries)
    kloc = split_heads(key_matrix)
    vloc = split_heads(values)
    cum = jnp.cumsum(log_decay, axis=1)
    last = cum[:, -1:]
    carry_decay = jnp.exp(last[:, 0])
    kscaled = kloc * jnp.exp(last - cum)[:, :, None]
    local_state = jnp.einsum("hjd,hje->hde", kscaled, vloc, precision=lax.Precision.HIGHEST)
    empty = jnp.zeros((heads_here, width, width), jnp.float32)
    _, state_in = prefix(
        (carry_decay, local_state), "seq", compose, (jnp.ones_like(carry_decay), empty)
    )
    lower = jnp.arange(rows)[:, None] >= jnp.arange(rows)[None, :]
    diff = cum[:, :, None] - cum[:, None, :]
    weight = jnp.where(lower[None], jnp.exp(jnp.where(lower[None], diff, 0.0)), 0.0)
    scores = jnp.einsum("hid,hjd->hij", qloc, kloc, precision=lax.Precision.HIGHEST) * weight
    inner = jnp.einsum("hij,hjd->hid", scores, vloc, precision=lax.Precision.HIGHEST)
    outer = jnp.exp(cum)[:, :, None] * jnp.einsum(
        "hid,hde->hie", qloc, state_in, precision=lax.Precision.HIGHEST
    )
    mixed = inner + outer
    mixed = mixed * lax.rsqrt(jnp.mean(mixed * mixed, axis=-1, keepdims=True) + 1e-06)
    attn = mixed.transpose(1, 0, 2).reshape(rows, heads_here * width).astype(jnp.bfloat16)
    stream = residual.astype(jnp.float32)
    normed = (stream * lax.rsqrt(jnp.mean(stream * stream, axis=-1, keepdims=True) + 1e-05)).astype(
        jnp.bfloat16
    )
    logits = jnp.dot(normed, router, preferred_element_type=jnp.float32)
    count_experts = router.shape[1]
    select_experts = (
        expert_ids[:, :, None] == jnp.arange(count_experts, dtype=jnp.int32)[None, None, :]
    )
    chosen = jnp.sum(jnp.where(select_experts, logits[:, None, :], 0.0), axis=-1)
    score = jax.nn.sigmoid(chosen)
    gates = score / jnp.sum(score, axis=1, keepdims=True)
    topk = expert_ids.shape[1]
    owner = lax.axis_index("exp")
    capacity = 3 * rows * topk // (2 * lax.axis_size("exp"))
    mine = (expert_ids.reshape(-1) == owner).astype(jnp.int32)
    ranks = jnp.cumsum(mine) - mine
    slot_pick = (ranks[None, :] == jnp.arange(capacity, dtype=jnp.int32)[:, None]) & (
        mine[None, :] == 1
    )
    slot_pick = slot_pick.astype(jnp.float32).reshape(capacity, rows, topk)
    token_pick = jnp.sum(slot_pick, axis=2).astype(jnp.bfloat16)
    slot_rows = jnp.dot(token_pick, normed, preferred_element_type=jnp.float32).astype(jnp.bfloat16)
    gathered_rows, full_weight = (
        lax.all_gather(slot_rows, "seq", axis=0, tiled=True),
        lax.all_gather(out_weight, "seq", axis=0, tiled=True),
    )
    projected = lax.dot_general(
        attn, full_weight, (((1,), (1,)), ((), ())), preferred_element_type=jnp.float32
    )
    hidden = jax.nn.silu(
        jnp.dot(gathered_rows, up_weight[0], preferred_element_type=jnp.float32)
    ).astype(jnp.bfloat16)
    expert_out = lax.psum_scatter(
        jnp.dot(hidden, down_weight[0], preferred_element_type=jnp.float32).astype(jnp.bfloat16),
        "seq",
        scatter_dimension=0,
        tiled=True,
    ).astype(jnp.float32)
    combine = jnp.einsum("cbk,bk->bc", slot_pick, gates, precision=lax.Precision.HIGHEST)
    contribution = jnp.dot(combine, expert_out, precision=lax.Precision.HIGHEST)
    summed = lax.psum_scatter(
        (projected + contribution).astype(jnp.bfloat16), "exp", scatter_dimension=0, tiled=True
    ).astype(jnp.float32)
    own_rows = summed.shape[0]
    own = lax.dynamic_slice_in_dim(stream, owner * own_rows, own_rows, 0)
    return (own + summed).astype(jnp.bfloat16)


def solution(mesh):
    in_specs = (
        P("seq", "exp"),
        P("seq", "exp"),
        P("seq", "exp"),
        P("exp", "seq"),
        P("seq", None),
        P("seq", "exp"),
        P(),
        P("seq", None),
        P("exp", None, "seq"),
        P("exp", "seq", None),
    )
    out_specs = P(("seq", "exp"), None)
    return jax.shard_map(shards, mesh=mesh, in_specs=in_specs, out_specs=out_specs, check_vma=False)
```

profile of v0, /device:TPU:0, one launch (start us, length us, event | category | flops | bytes accessed | tf_op | source)
XLA Modules:
  0.0 169.6 jit_solution(17992035353108971294)
XLA Ops:
  6.5 0.7 broadcast_compare_fusion
  7.3 0.1 copy.56
  7.4 0.1 reshape.171
  7.5 0.3 reduce-window.9
  7.8 0.1 reshape.166
  8.0 0.1 slice.14
  8.0 0.1 copy.57
  8.1 0.1 slice_reduce_fusion
  8.3 0.1 broadcast.95
  8.3 0.1 reshape.168
  8.4 1.4 multiply_reduce_fusion
  9.8 2.2 %convolution_convert_fusion = bf16[48,3072]{1,0:T(8,128)(2,1)} fusion(f32[128]{0:T(128)S(1)} %add_rsqrt_fusion, bf16[128,3072]{1,0:T(8,128)(2,1)} %param.16, bf16[48,128]{1,0:T(8,128)(2,1)S(1)} %convert_reduce_fusion), kind=kOutput, calls=%fused_computation.10 | convolution fusion | flops 39075840 | bytes 1094144 | tf_op jit(solution)/shard_map/dot_general | solution.py:94
  12.1 0.0 all-gather.7.cloned.1.call-update
  12.1 0.0 reduce-scatter.3.cloned.1.call-start
  12.1 33.2 %all-gather.7.cloned.1.call-done = bf16[192,3072]{1,0:T(8,128)(2,1)} async-done(((bf16[48,3072]{1,0:T(8,128)(2,1)}), bf16[192,3072]{1,0:T(8,128)(2,1)}) %all-gather.7.cloned.1.call-update) | async-done | bytes 1179664 | tf_op jit(solution)/shard_map/all_gather | solution.py:96
  45.4 9.6 %fusion.5 = bf16[192,3072]{1,0:T(8,128)(2,1)} fusion(bf16[1,1152,3072]{2,1,0:T(8,128)(2,1)} %param.21, bf16[192,3072]{1,0:T(8,128)(2,1)} %all-gather.7.cloned.1.call-done, bf16[1,3072,1152]{2,1,0:T(8,128)(2,1)} %param.20), kind=kOutput, calls=%fused_computation.7 | convolution fusion | flops 2719604736 | bytes 16515072 | tf_op jit(solution)/shard_map/dot_general | solution.py:106
  55.0 0.0 reduce-scatter.3.cloned.1.call-update
  55.1 0.0 all-gather.5.cloned.1.call-start
  55.1 0.7 all-gather.5.cloned.1.call-update
  55.8 0.0 reduce-scatter.5.cloned.1.call-start
  55.9 0.3 reduce_window_sum.27
  56.2 0.2 slice_reduce_fusion.1
  56.3 0.2 fusion.32
  56.6 0.1 exponential_bitcast_fusion
  56.6 0.1 copy.68
  56.8 0.2 convolution_convert_fusion.1
  57.0 16.0 %all-gather.1 = bf16[8,128,128]{2,1,0:T(8,128)(2,1)S(1)} all-gather(bf16[2,128,128]{2,1,0:T(8,128)(2,1)S(1)} %convolution_convert_fusion.1), channel_id=3, replica_groups=mesh['seq'=4,'exp'=8] {'seq'}, dimensions={0}, use_global_device_ids=true | all-gather | bytes 327680 | tf_op jit(solution)/shard_map/all_gather | solution.py:10
  72.9 0.6 dynamic-slice
  74.2 0.2 dynamic-update-slice
  74.4 10.5 %all-reduce = bf16[8]{0:T(256)(128)(2,1)S(1)} all-reduce(bf16[8]{0:T(256)(128)(2,1)S(1)} %dynamic-update-slice), channel_id=2, replica_groups=mesh['seq'=4,'exp'=8] {'seq'}, use_global_device_ids=true, to_apply=%add | all-reduce | flops 8 | bytes 32
  84.9 0.1 reshape.172
  85.0 0.4 fusion.14
  85.5 0.2 convolution_multiply_fusion
  85.7 0.5 while.14
  85.7 0.1 fusion.50
  85.8 0.1 fusion.50
  85.9 0.1 fusion.50
  86.1 0.1 fusion.50
  86.2 0.3 fusion.23
  86.5 0.3 fusion.16
  86.8 0.0 reduce-scatter.3.cloned.1.call-done
  86.8 1.8 %fusion.34 = f32[128,3072]{1,0:T(8,128)S(1)} fusion(f32[128,48]{0,1:T(8,128)S(1)} %select_reduce_fusion, bf16[48,3072]{1,0:T(8,128)(2,1)} %reduce-scatter.3.cloned.1.call-done), kind=kOutput, calls=%fused_computation.61 | convolution fusion | flops 226492416 | bytes 1892352 | tf_op jit(solution)/shard_map/dot_general | solution.py:112
  88.6 35.9 %all-gather.5.cloned.1.call-done = bf16[3072,256]{1,0:T(8,128)(2,1)} async-done(((bf16[768,256]{1,0:T(8,128)(2,1)}), bf16[3072,256]{1,0:T(8,128)(2,1)}) %all-gather.5.cloned.1.call-update) | async-done | bytes 1572880 | tf_op jit(solution)/shard_map/all_gather | solution.py:97
  124.5 3.0 %fusion.8 = bf16[128,3072]{1,0:T(8,128)(2,1)} fusion(f32[128,3072]{1,0:T(8,128)S(1)} %fusion.34, bf16[128,256]{0,1:T(8,128)(2,1)S(1)} %bitcast.99, bf16[3072,256]{1,0:T(8,128)(2,1)} %all-gather.5.cloned.1.call-done), kind=kOutput, calls=%fused_computation.9 | convolution fusion | flops 202113024 | bytes 3997696 | tf_op jit(solution)/shard_map/dot_general | solution.py:99
  127.5 0.0 reduce-scatter.5.cloned.1.call-update
  127.5 0.1 convert_element_type.97
  127.7 33.9 %reduce-scatter.5.cloned.1.call-done = bf16[16,3072]{1,0:T(8,128)(2,1)} async-done(((bf16[128,3072]{1,0:T(8,128)(2,1)}), bf16[16,3072]{1,0:T(8,128)(2,1)}) %reduce-scatter.5.cloned.1.call-update) | async-done | bytes 98320 | tf_op jit(solution)/shard_map/reduce_scatter | solution.py:113
  161.5 1.6 add_convert_fusion
  (34 shorter events, 0.3 us)
Async XLA Ops:
  6.5 50.2 %copy-start = (bf16[128,256]{1,0:T(8,128)(2,1)S(1)}, bf16[128,256]{1,0:T(8,128)(2,1)}, u32[]{:S(2)}) copy-start(bf16[128,256]{1,0:T(8,128)(2,1)} %param.14) | copy-start | bytes 196612
  6.5 38.8 %all-gather.7.cloned.1.call-start = ((), (), s32[]{:S(2)}) async-start(), calls=%async_computation.3 | async-start | bytes 1474560 | tf_op jit(solution)/shard_map/all_gather | solution.py:96
  12.1 74.7 %reduce-scatter.3.cloned.1.call-start = ((), (), s32[]{:S(2)}) async-start(), calls=%async_computation.4 | async-start | bytes 1474560 | tf_op jit(solution)/shard_map/reduce_scatter | solution.py:105
  55.0 0.9 copy-start.5
  55.0 1.7 copy-start.3
  55.0 18.0 %copy-start.7 = (u32[32]{0:T(128)S(1)}, u32[32]{0:T(128)}, u32[]{:S(2)}) copy-start(u32[32]{0:T(128)} %constant.66) | copy-start | bytes 388
  55.0 30.0 %copy-start.1 = (bf16[128,3072]{1,0:T(8,128)(2,1)S(1)}, bf16[128,3072]{1,0:T(8,128)(2,1)}, u32[]{:S(2)}) copy-start(bf16[128,3072]{1,0:T(8,128)(2,1)} %param.16) | copy-start | bytes 2359300
  55.0 30.0 %copy-start.6 = (bf16[3072,8]{0,1:T(8,128)(2,1)S(1)}, bf16[3072,8]{0,1:T(8,128)(2,1)}, u32[]{:S(2)}) copy-start(bf16[3072,8]{0,1:T(8,128)(2,1)} %param.18) | copy-start | bytes 147460
  55.0 30.4 %copy-start.4 = (s32[128,2]{0,1:T(2,128)S(1)}, s32[128,2]{0,1:T(2,128)}, u32[]{:S(2)}) copy-start(s32[128,2]{0,1:T(2,128)} %param.19) | copy-start | bytes 3076
  55.0 30.5 %copy-start.2 = (bf16[128,256]{1,0:T(8,128)(2,1)S(1)}, bf16[128,256]{1,0:T(8,128)(2,1)}, u32[]{:S(2)}) copy-start(bf16[128,256]{1,0:T(8,128)(2,1)} %param.12) | copy-start | bytes 196612
  55.1 69.5 %all-gather.5.cloned.1.call-start = ((), (), s32[]{:S(2)}) async-start(), calls=%async_computation.2 | async-start | bytes 1966080 | tf_op jit(solution)/shard_map/all_gather | solution.py:97
  55.8 105.7 %reduce-scatter.5.cloned.1.call-start = ((), (), s32[]{:S(2)}) async-start(), calls=%async_computation.5 | async-start | bytes 884736 | tf_op jit(solution)/shard_map/reduce_scatter | solution.py:113
Sparse Core Ops, SparseCore 0:
  12.2 33.1 all-gather.6
  55.2 31.1 reduce-scatter.2
  88.0 36.4 all-gather.4
  127.6 33.8 reduce-scatter.4
where the time goes:
time: 170 us
  waiting for transfers between devices  104 us (61%)
  blocking collectives  26.4 us (16%)
  matrix products  17.9 us (11%)
  between operations  14 us (8%)
  other arithmetic  5.26 us (3%)
  local copies, waits for them, and re-layouts  2.07 us (1%)
    all_gather x1, waiting for transfers between devices, shards(): lax.all_gather(out_weight, 'seq', axis=0, tiled=True)  35.9 us
    reduce_scatter x1, waiting for transfers between devices, shards(): lax.psum_scatter((projected + contribution).astype(jnp.bfloat16), 'exp',...  33.9 us
    all_gather x1, waiting for transfers between devices, shards(): lax.all_gather(slot_rows, 'seq', axis=0, tiled=True)  33.2 us
    all_gather x1, blocking collectives, prefix(): lax.all_gather(part.astype(kind), axis)  16 us
    unnamed x1, blocking collectives  10.5 us
    dot_general x1, matrix products, shards(): jnp.dot(hidden, down_weight[0], preferred_element_type=jnp.float32)  9.6 us
  transfers between devices with their start and end apart: 4, of which 3 were waited for; matrix products, arithmetic and copies ran while one was open for 3% of the time, Pallas kernels for 0%

commit v1 on v0

v1 whole, which is shorter than its diff:
```python
import functools

import jax
import jax.numpy as jnp
from jax import lax
from jax.experimental import pallas as pl
from jax.experimental.pallas import tpu as pltpu
from jax.sharding import PartitionSpec as P

MESH = pl.DeviceIdType.MESH
F32 = jnp.float32
BF16 = jnp.bfloat16
EXACT = lax.Precision.HIGHEST


def tile_of(size, most):
    for width in range(most, 127, -128):
        if size % width == 0:
            return width
    return size


def layer(
    n,
    n_exp,
    cap,
    q_ref,
    k_ref,
    v_ref,
    decay_ref,
    res_ref,
    ow_ref,
    router_ref,
    ids_ref,
    up_hbm,
    down_hbm,
    out_ref,
    up,
    down,
    rows_buf,
    hidden,
    states,
    carried,
    attn_buf,
    stage,
    core_buf,
    half_buf,
    chip_buf,
    fin_send,
    fin_buf,
    load_sem,
    rows_s,
    rows_r,
    st_s,
    st_r,
    at_s,
    at_r,
    core_s,
    core_r,
    chip_s,
    chip_r,
    fin_s,
    fin_r,
):
    s = lax.axis_index("seq")
    e = lax.axis_index("exp")
    core = e % 2
    chip = e // 2
    chips = n_exp // 2
    partner = chip * 2 + 1 - core
    blk, width_d = res_ref.shape
    own = blk // n_exp
    heads = decay_ref.shape[0]
    dh = q_ref.shape[1] // heads
    cols = ow_ref.shape[0]

    load_up = pltpu.make_async_copy(up_hbm.at[0], up, load_sem.at[0])
    load_down = pltpu.make_async_copy(down_hbm.at[0], down, load_sem.at[1])
    load_up.start()
    load_down.start()

    barrier = pltpu.get_barrier_semaphore()

    @pl.loop(0, n)
    def _(j):
        @pl.when(j != s)
        def _():
            pl.semaphore_signal(barrier, inc=1, device_id=(j, e), device_id_type=MESH)

    @pl.loop(0, chips)
    def _(g):
        @pl.when(g != chip)
        def _():
            pl.semaphore_signal(
                barrier, inc=1, device_id=(s, g * 2 + core), device_id_type=MESH
            )

    pl.semaphore_signal(barrier, inc=1, device_id=(s, partner), device_id_type=MESH)

    def send_rows(b, way):
        return pltpu.make_async_remote_copy(
            src_ref=rows_buf.at[b],
            dst_ref=rows_buf.at[b],
            send_sem=rows_s.at[way, b],
            recv_sem=rows_r.at[b],
            device_id=((s + 1) % n if way == 0 else (s + n - 1) % n, e),
            device_id_type=MESH,
        )

    def send_state(to, slot):
        return pltpu.make_async_remote_copy(
            src_ref=states.at[slot],
            dst_ref=states.at[slot],
            send_sem=st_s.at[to],
            recv_sem=st_r.at[slot],
            device_id=(to, e),
            device_id_type=MESH,
        )

    def send_attn(to, slot):
        return pltpu.make_async_remote_copy(
            src_ref=attn_buf.at[slot],
            dst_ref=attn_buf.at[slot],
            send_sem=at_s.at[to],
            recv_sem=at_r.at[slot],
            device_id=(to, e),
            device_id_type=MESH,
        )

    def send_core(t):
        return pltpu.make_async_remote_copy(
            src_ref=stage.at[t, 1 - core],
            dst_ref=core_buf.at[t],
            send_sem=core_s.at[t],
            recv_sem=core_r.at[t],
            device_id=(s, partner),
            device_id_type=MESH,
        )

    def send_chip(t, to, slot):
        return pltpu.make_async_remote_copy(
            src_ref=half_buf.at[t, to],
            dst_ref=chip_buf.at[t, slot],
            send_sem=chip_s.at[t, to],
            recv_sem=chip_r.at[t, slot],
            device_id=(s, to * 2 + core),
            device_id_type=MESH,
        )

    def send_fin(t, to, slot):
        return pltpu.make_async_remote_copy(
            src_ref=fin_send.at[t],
            dst_ref=fin_buf.at[slot],
            send_sem=fin_s.at[t],
            recv_sem=fin_r.at[slot],
            device_id=(to, e),
            device_id_type=MESH,
        )

    stream = res_ref[...].astype(F32)
    normed = (
        stream * lax.rsqrt(jnp.mean(stream * stream, axis=-1, keepdims=True) + 1e-05)
    ).astype(BF16)
    logits = jnp.dot(normed, router_ref[...], preferred_element_type=F32)
    ids = ids_ref[...]
    which = lax.broadcasted_iota(jnp.int32, logits.shape, 1)
    scores = []
    for k in range(ids.shape[1]):
        chosen = jnp.sum(
            jnp.where(ids[:, k : k + 1] == which, logits, 0.0), axis=1, keepdims=True
        )
        scores.append(1.0 / (1.0 + jnp.exp(-chosen)))
    total = functools.reduce(lambda a, b: a + b, scores)
    gate = jnp.zeros((blk, 1), F32)
    mine = jnp.zeros((blk, 1), F32)
    for k, score in enumerate(scores):
        hit = ids[:, k : k + 1] == e
        gate = gate + jnp.where(hit, score / total, 0.0)
        mine = mine + jnp.where(hit, 1.0, 0.0)
    row_i = lax.broadcasted_iota(jnp.int32, (blk, blk), 0)
    col_i = lax.broadcasted_iota(jnp.int32, (blk, blk), 1)
    mine_t = jnp.broadcast_to(mine, (blk, blk)).T
    gate_t = jnp.broadcast_to(gate, (blk, blk)).T
    before = jnp.where(row_i < col_i, 1.0, 0.0).astype(BF16)
    rank = jnp.dot(mine_t.astype(BF16), before, preferred_element_type=F32)
    pick = jnp.where(
        (rank.astype(jnp.int32) == row_i) & (mine_t > 0.5), 1.0, 0.0
    )[:cap]
    comb = pick * gate_t[:cap]
    comb_hi = comb.astype(BF16)
    comb_lo = (comb - comb_hi.astype(F32)).astype(BF16)
    rows_buf[s, :, :width_d] = jnp.dot(
        pick.astype(BF16), normed, preferred_element_type=F32
    ).astype(BF16)
    rows_buf[s, :, width_d : width_d + blk] = comb_hi
    rows_buf[s, :, width_d + blk : width_d + 2 * blk] = comb_lo

    pl.semaphore_wait(barrier, n - 1 + chips)

    def forward(b):
        @pl.when((b <= s) & (s < n - 1))
        def _():
            send_rows(b, 0).start()

        @pl.when((b >= s) & (s > 0))
        def _():
            send_rows(b, 1).start()

    forward(s)

    lower = row_i >= col_i
    for h in range(heads):
        lanes = slice(h * dh, (h + 1) * dh)
        g = jnp.broadcast_to(decay_ref[h : h + 1, :], (blk, blk))
        cum = jnp.sum(jnp.where(lower, g, 0.0), axis=1, keepdims=True)
        last = cum[blk - 1 : blk, :]
        scaled = k_ref[:, lanes].astype(F32) * jnp.exp(last - cum)
        local = jnp.dot(
            scaled.T, v_ref[:, lanes].astype(F32), precision=EXACT, preferred_element_type=F32
        )
        states[s, h, :dh, :] = local.astype(BF16)
        states[s, h, dh:, :] = jnp.broadcast_to(jnp.exp(last), (16, dh)).astype(BF16)

    @pl.loop(0, n)
    def _(j):
        @pl.when(j > s)
        def _():
            send_state(j, s).start()

    carried[...] = jnp.zeros_like(carried)

    @pl.loop(0, n)
    def _(j):
        @pl.when(j < s)
        def _():
            send_state(j, j).wait_recv()
            for h in range(heads):
                carried[h] = (
                    states[j, h, dh : dh + 16, :].astype(F32)[0:1, :] * carried[h]
                    + states[j, h, :dh, :].astype(F32)
                )

    for h in range(heads):
        lanes = slice(h * dh, (h + 1) * dh)
        g = jnp.broadcast_to(decay_ref[h : h + 1, :], (blk, blk))
        cum = jnp.sum(jnp.where(lower, g, 0.0), axis=1, keepdims=True)
        diff = cum - jnp.broadcast_to(cum, (blk, blk)).T
        weight = jnp.where(lower, jnp.exp(jnp.where(lower, diff, 0.0)), 0.0)
        q = q_ref[:, lanes]
        sc = (
            lax.dot_general(
                q, k_ref[:, lanes], (((1,), (1,)), ((), ())), preferred_element_type=F32
            )
            * weight
        )
        mixed = jnp.dot(
            sc, v_ref[:, lanes].astype(F32), precision=EXACT, preferred_element_type=F32
        ) + jnp.exp(cum) * jnp.dot(
            q.astype(F32), carried[h], precision=EXACT, preferred_element_type=F32
        )
        mixed = mixed * lax.rsqrt(jnp.mean(mixed * mixed, axis=-1, keepdims=True) + 1e-06)
        attn_buf[s, :, lanes] = mixed.astype(BF16)

    @pl.loop(0, n)
    def _(j):
        @pl.when(j != s)
        def _():
            send_attn(j, s).start()

    load_up.wait()
    load_down.wait()

    near = jnp.minimum(s, n - 1 - s)
    toward = jnp.where(s > n - 1 - s, -1, 1)

    def block_of(t):
        alternate = s + jnp.where(t % 2 == 1, -((t + 1) // 2), t // 2)
        return jnp.where(t <= 2 * near, alternate, s + toward * (t - near))

    def arrive(t):
        b = block_of(t)
        send_rows(b, 0).wait_recv()
        forward(b)

    up_tile = tile_of(up.shape[1], 384)
    down_tile = tile_of(width_d, 512)

    def compute(t, b):
        x = rows_buf[b, :, :width_d]
        for c in range(0, up.shape[1], up_tile):
            z = jnp.dot(x, up[:, c : c + up_tile], preferred_element_type=F32)
            hidden[:, c : c + up_tile] = (z / (1.0 + jnp.exp(-z))).astype(BF16)
        hi = rows_buf[b, :, width_d : width_d + blk]
        lo = rows_buf[b, :, width_d + blk : width_d + 2 * blk]
        pair = jnp.concatenate([hi, lo], axis=0).astype(F32).T.astype(BF16)
        hid = hidden[...]

        @pl.when(t > 0)
        def _():
            send_attn(b, b).wait_recv()

        proj = lax.dot_general(
            attn_buf[b], ow_ref[...], (((1,), (1,)), ((), ())), preferred_element_type=F32
        )
        for c in range(0, width_d, down_tile):
            o = jnp.dot(hid, down[:, c : c + down_tile], preferred_element_type=F32).astype(BF16)
            both = jnp.concatenate([o, o], axis=0)
            y = jnp.dot(pair, both, preferred_element_type=F32).astype(BF16)
            for g in range(n_exp):
                stage[t, g % 2, g // 2, :, c : c + down_tile] = y[g * own : (g + 1) * own]
        if cols % 128 == 0:
            at = pl.ds(pl.multiple_of(s * cols, 128), cols)
            for g in range(n_exp):
                part = stage[t, g % 2, g // 2, :, at].astype(F32)
                stage[t, g % 2, g // 2, :, at] = (part + proj[g * own : (g + 1) * own]).astype(BF16)
        else:
            for j in range(n):

                @pl.when(s == j)
                def _():
                    at = slice(j * cols, (j + 1) * cols)
                    for g in range(n_exp):
                        part = stage[t, g % 2, g // 2, :, at].astype(F32)
                        stage[t, g % 2, g // 2, :, at] = (
                            part + proj[g * own : (g + 1) * own]
                        ).astype(BF16)

    def across_cores(t):
        send_core(t).wait_recv()

        @pl.loop(0, chips)
        def _(g):
            half_buf[t, g] = (
                stage[t, core, g].astype(F32) + core_buf[t, g].astype(F32)
            ).astype(BF16)

            @pl.when(g != chip)
            def _():
                send_chip(t, g, chip).start()

    def across_chips(t):
        chip_buf[t, chip] = half_buf[t, chip]

        @pl.loop(0, chips)
        def _(g):
            @pl.when(g != chip)
            def _():
                send_chip(t, g, g).wait_recv()

        acc = chip_buf[t, 0].astype(F32)
        for g in range(1, chips):
            acc = acc + chip_buf[t, g].astype(F32)
        fin_send[t] = acc.astype(BF16)

        @pl.when(t > 0)
        def _():
            send_fin(t, block_of(t), s).start()

    @pl.loop(0, n)
    def _(t):
        @pl.when(t % 2 == 1)
        def _():
            arrive(t)

            @pl.when(t + 1 <= 2 * near)
            def _():
                arrive(t + 1)

        @pl.when((t % 2 == 0) & (t > 2 * near) & (t > 0))
        def _():
            arrive(t)

        compute(t, block_of(t))
        send_core(t).start()

        @pl.when(t > 0)
        def _():
            across_chips(t - 1)

        across_cores(t)

    across_chips(n - 1)
    picked = jnp.where(
        lax.broadcasted_iota(jnp.int32, (max(own, 16), blk), 1)
        == lax.broadcasted_iota(jnp.int32, (max(own, 16), blk), 0) + e * own,
        1.0,
        0.0,
    ).astype(BF16)
    base = jnp.dot(picked, res_ref[...], preferred_element_type=F32)[:own]
    fin_buf[s] = fin_send[0]

    @pl.loop(0, n)
    def _(j):
        @pl.when(j != s)
        def _():
            send_fin(0, j, j).wait_recv()

    acc = fin_buf[0].astype(F32)
    for j in range(1, n):
        acc = acc + fin_buf[j].astype(F32)
    out_ref[...] = (base + acc).astype(BF16)

    @pl.loop(0, n)
    def _(j):
        @pl.when((j <= s) & (s < n - 1))
        def _():
            send_rows(j, 0).wait_send()

        @pl.when((j >= s) & (s > 0))
        def _():
            send_rows(j, 1).wait_send()

        @pl.when(j > s)
        def _():
            send_state(j, s).wait_send()

        @pl.when(j != s)
        def _():
            send_attn(j, s).wait_send()

        send_core(j).wait_send()

        @pl.when(j > 0)
        def _():
            send_fin(j, block_of(j), s).wait_send()

        @pl.loop(0, chips)
        def _(g):
            @pl.when(g != chip)
            def _():
                send_chip(j, g, chip).wait_send()


def shards(
    queries,
    key_matrix,
    values,
    log_decay,
    residual,
    out_weight,
    router,
    expert_ids,
    up_weight,
    down_weight,
):
    n = lax.axis_size("seq")
    n_exp = lax.axis_size("exp")
    blk, width_d = residual.shape
    heads = log_decay.shape[0]
    feats = queries.shape[1]
    dh = feats // heads
    cap = 3 * blk * expert_ids.shape[1] // (2 * n_exp)
    cap = -(-cap // 16) * 16
    own = blk // n_exp
    chips = n_exp // 2
    ff = up_weight.shape[2]
    dma = pltpu.SemaphoreType.DMA
    vmem = pl.BlockSpec(memory_space=pltpu.VMEM)
    hbm = pl.BlockSpec(memory_space=pl.ANY)
    return pl.pallas_call(
        functools.partial(layer, n, n_exp, cap),
        out_shape=jax.ShapeDtypeStruct((own, width_d), BF16),
        in_specs=[vmem] * 8 + [hbm] * 2,
        out_specs=vmem,
        scratch_shapes=[
            pltpu.VMEM((width_d, ff), BF16),
            pltpu.VMEM((ff, width_d), BF16),
            pltpu.VMEM((n, cap, width_d + 2 * blk), BF16),
            pltpu.VMEM((cap, ff), BF16),
            pltpu.VMEM((n, heads, dh + 16, dh), BF16),
            pltpu.VMEM((heads, dh, dh), F32),
            pltpu.VMEM((n, blk, feats), BF16),
            pltpu.VMEM((n, 2, chips, own, width_d), BF16),
            pltpu.VMEM((n, chips, own, width_d), BF16),
            pltpu.VMEM((n, chips, own, width_d), BF16),
            pltpu.VMEM((n, chips, own, width_d), BF16),
            pltpu.VMEM((n, own, width_d), BF16),
            pltpu.VMEM((n, own, width_d), BF16),
            dma((2,)),
            dma((2, n)),
            dma((n,)),
            dma((n,)),
            dma((n,)),
            dma((n,)),
            dma((n,)),
            dma((n,)),
            dma((n,)),
            dma((n, chips)),
            dma((n, chips)),
            dma((n,)),
            dma((n,)),
        ],
        compiler_params=pltpu.CompilerParams(
            collective_id=0,
            has_side_effects=True,
            vmem_limit_bytes=56 * 2**20,
        ),
    )(
        queries,
        key_matrix,
        values,
        log_decay,
        residual,
        out_weight,
        router,
        expert_ids,
        up_weight,
        down_weight,
    )


def solution(mesh):
    in_specs = (
        P("seq", "exp"),
        P("seq", "exp"),
        P("seq", "exp"),
        P("exp", "seq"),
        P("seq", None),
        P("seq", "exp"),
        P(),
        P("seq", None),
        P("exp", None, "seq"),
        P("exp", "seq", None),
    )
    out_specs = P(("seq", "exp"), None)
    return jax.shard_map(shards, mesh=mesh, in_specs=in_specs, out_specs=out_specs, check_vma=False)
```

time: 170 us -> 70 us (0.41)
  waiting for transfers between devices: 104 us -> 0 us
  Pallas kernels: 0 us -> 64.8 us
  blocking collectives: 26.4 us -> 0 us
  matrix products: 17.9 us -> 0 us
  between operations: 14 us -> 0.01 us
  other arithmetic: 5.26 us -> 0 us
  local copies, waits for them, and re-layouts: 2.07 us -> 4.9 us
    all_gather x2 -> x0, waiting for transfers between devices: 69.1 us -> none  [the longest x1 35.9 us: shards(): lax.all_gather(out_weight, 'seq', axis=0, tiled=True)]
    pallas_call x0 -> x1, Pallas kernels: none -> 64.8 us  [shards(): pl.pallas_call(functools.partial(layer, n, n_exp, cap), out_shape=jax.Sha...]
    reduce_scatter x2 -> x0, waiting for transfers between devices: 33.9 us -> none  [the longest x1 33.9 us: shards(): lax.psum_scatter((projected + contribution).astype(jnp.bfloat16), 'exp',...]
    dot_general x9 -> x0, matrix products: 17.9 us -> none  [the longest x1 9.6 us: shards(): jnp.dot(hidden, down_weight[0], preferred_element_type=jnp.float32)]
    all_gather x1 -> x0, blocking collectives: 16 us -> none  [prefix(): lax.all_gather(part.astype(kind), axis)]
    unnamed x1 -> x0, blocking collectives: 10.5 us -> none
    unnamed x19 -> x3, local copies, waits for them, and re-layouts: 0.87 us -> 4.9 us
    convert_element_type x8 -> x0, other arithmetic: 1.94 us -> none  [the longest x1 1.55 us: shards(): return (own + summed).astype(jnp.bfloat16)]
  transfers between devices with their start and end apart: 4 -> 0, of which waited for: 3 -> 0; matrix products, arithmetic and copies ran while one was open for 3% -> 0% of each run, Pallas kernels for 0% -> 0%
where the time goes in v1:
time: 70 us; the launch traced here: 69.7 us
  Pallas kernels  64.8 us (93%)
  local copies, waits for them, and re-layouts  4.9 us (7%)
    pallas_call x1, Pallas kernels, shards(): pl.pallas_call(functools.partial(layer, n, n_exp, cap), out_shape=jax.Sha...  64.8 us
    unnamed x3, local copies, waits for them, and re-layouts  4.9 us

profile of v1, /device:TPU:0, one launch (start us, length us, event | category | flops | bytes accessed | tf_op | source)
XLA Modules:
  0.0 69.7 jit_solution(14555674122629492626)
XLA Ops:
  0.0 1.4 %copy.12.ids_ref = s32[128,2]{1,0:T(8,128)} copy(s32[128,2]{0,1:T(2,128)} %param.17) | data formatting | bytes 2048 | tf_op args[7]
  1.4 2.0 %copy.11.router_ref = bf16[3072,8]{1,0:T(8,128)(2,1)} copy(bf16[3072,8]{0,1:T(8,128)(2,1)} %param.16) | data formatting | bytes 98304 | tf_op args[6]
  3.4 64.8 %shard_map.100 = bf16[16,3072]{1,0:T(8,128)(2,1)} custom-call(bf16[128,256]{1,0:T(8,128)(2,1)} %q_ref.1, bf16[128,256]{1,0:T(8,128)(2,1)} %k_ref.1, bf16[128,256]{1,0:T(8,128)(2,1)} %v_ref.1, f32[2,128]{1,0:T(2,128)} %decay_ref.1, bf16[128,3072]{1,0:T(8,128)(2,1)} %res_ref.1, bf16[768,256]{1,0:T(8,128)(2,1)} %ow_ref.1, bf16[3072,8]{1,0:T(8,128)(2,1)} %copy.11.router_ref, ...), custom_call_target="tpu_custom_call" | custom-call | tf_op jit(solution)/shard_map/pallas_call | solution.py:460
  68.2 1.5 %copy.14 = bf16[16,3072]{1,0:T(8,128)(2,1)} copy(bf16[16,3072]{1,0:T(8,128)(2,1)} %shard_map.100) | data formatting | bytes 196608

commit v2 on v1

--- a/solution.py
+++ b/solution.py
@@ -161,26 +161,28 @@
     normed = (
         stream * lax.rsqrt(jnp.mean(stream * stream, axis=-1, keepdims=True) + 1e-05)
     ).astype(BF16)
-    logits = jnp.dot(normed, router_ref[...], preferred_element_type=F32)
+    logits = lax.dot_general(
+        router_ref[...], normed, (((1,), (1,)), ((), ())), preferred_element_type=F32
+    )
     ids = ids_ref[...]
-    which = lax.broadcasted_iota(jnp.int32, logits.shape, 1)
+    which = lax.broadcasted_iota(jnp.int32, logits.shape, 0)
     scores = []
-    for k in range(ids.shape[1]):
+    for k in range(ids.shape[0]):
         chosen = jnp.sum(
-            jnp.where(ids[:, k : k + 1] == which, logits, 0.0), axis=1, keepdims=True
+            jnp.where(ids[k : k + 1, :] == which, logits, 0.0), axis=0, keepdims=True
         )
         scores.append(1.0 / (1.0 + jnp.exp(-chosen)))
     total = functools.reduce(lambda a, b: a + b, scores)
-    gate = jnp.zeros((blk, 1), F32)
-    mine = jnp.zeros((blk, 1), F32)
+    gate = jnp.zeros((1, blk), F32)
+    mine = jnp.zeros((1, blk), F32)
     for k, score in enumerate(scores):
-        hit = ids[:, k : k + 1] == e
+        hit = ids[k : k + 1, :] == e
         gate = gate + jnp.where(hit, score / total, 0.0)
         mine = mine + jnp.where(hit, 1.0, 0.0)
     row_i = lax.broadcasted_iota(jnp.int32, (blk, blk), 0)
     col_i = lax.broadcasted_iota(jnp.int32, (blk, blk), 1)
-    mine_t = jnp.broadcast_to(mine, (blk, blk)).T
-    gate_t = jnp.broadcast_to(gate, (blk, blk)).T
+    mine_t = jnp.broadcast_to(mine, (blk, blk))
+    gate_t = jnp.broadcast_to(gate, (blk, blk))
     before = jnp.where(row_i < col_i, 1.0, 0.0).astype(BF16)
     rank = jnp.dot(mine_t.astype(BF16), before, preferred_element_type=F32)
     pick = jnp.where(
@@ -227,6 +229,18 @@
         def _():
             send_state(j, s).start()
 
+    up_tile = tile_of(up.shape[1], 384)
+    down_tile = tile_of(width_d, 512)
+
+    def expand(b):
+        x = rows_buf[b, :, :width_d]
+        for c in range(0, up.shape[1], up_tile):
+            z = jnp.dot(x, up[:, c : c + up_tile], preferred_element_type=F32)
+            hidden[:, c : c + up_tile] = (z / (1.0 + jnp.exp(-z))).astype(BF16)
+
+    load_up.wait()
+    expand(s)
+
     carried[...] = jnp.zeros_like(carried)
 
     @pl.loop(0, n)
@@ -267,7 +281,6 @@
         def _():
             send_attn(j, s).start()
 
-    load_up.wait()
     load_down.wait()
 
     near = jnp.minimum(s, n - 1 - s)
@@ -282,14 +295,12 @@
         send_rows(b, 0).wait_recv()
         forward(b)
 
-    up_tile = tile_of(up.shape[1], 384)
-    down_tile = tile_of(width_d, 512)
-
     def compute(t, b):
-        x = rows_buf[b, :, :width_d]
-        for c in range(0, up.shape[1], up_tile):
-            z = jnp.dot(x, up[:, c : c + up_tile], preferred_element_type=F32)
-            hidden[:, c : c + up_tile] = (z / (1.0 + jnp.exp(-z))).astype(BF16)
+        @pl.when(t > 0)
+        def _():
+            expand(b)
+            across_cores(t - 1)
+
         hi = rows_buf[b, :, width_d : width_d + blk]
         lo = rows_buf[b, :, width_d + blk : width_d + 2 * blk]
         pair = jnp.concatenate([hi, lo], axis=0).astype(F32).T.astype(BF16)
@@ -373,12 +384,12 @@
         compute(t, block_of(t))
         send_core(t).start()
 
-        @pl.when(t > 0)
+        @pl.when((t > 0) & (t < n - 1))
         def _():
             across_chips(t - 1)
 
-        across_cores(t)
-
+    across_cores(n - 1)
+    across_chips(n - 2)
     across_chips(n - 1)
     picked = jnp.where(
         lax.broadcasted_iota(jnp.int32, (max(own, 16), blk), 1)
@@ -502,8 +513,8 @@
         log_decay,
         residual,
         out_weight,
-        router,
-        expert_ids,
+        router.T,
+        expert_ids.T,
         up_weight,
         down_weight,
     )

time: 70 us -> 65.7 us (0.939)
  local copies, waits for them, and re-layouts: 4.9 us -> 1.54 us
  Pallas kernels: 64.8 us -> 64 us
    unnamed x3 -> x1, local copies, waits for them, and re-layouts: 4.9 us -> 1.54 us
    pallas_call x1, Pallas kernels: 64.8 us -> 64 us  [shards(): pl.pallas_call(functools.partial(layer, n, n_exp, cap), out_shape=jax.Sha...]
where the time goes in v2:
time: 65.7 us; the launch traced here: 65.5 us
  Pallas kernels  64 us (97%)
  local copies, waits for them, and re-layouts  1.54 us (2%)
    pallas_call x1, Pallas kernels, shards(): pl.pallas_call(functools.partial(layer, n, n_exp, cap), out_shape=jax.Sha...  64 us
    unnamed x1, local copies, waits for them, and re-layouts  1.54 us

profile of v2, /device:TPU:0, one launch (start us, length us, event | category | flops | bytes accessed | tf_op | source)
XLA Modules:
  0.0 65.5 jit_solution(6117428844689895000)
XLA Ops:
  0.0 64.0 %shard_map.100 = bf16[16,3072]{1,0:T(8,128)(2,1)} custom-call(bf16[128,256]{1,0:T(8,128)(2,1)} %q_ref.1, bf16[128,256]{1,0:T(8,128)(2,1)} %k_ref.1, bf16[128,256]{1,0:T(8,128)(2,1)} %v_ref.1, f32[2,128]{1,0:T(2,128)} %decay_ref.1, bf16[128,3072]{1,0:T(8,128)(2,1)} %res_ref.1, bf16[768,256]{1,0:T(8,128)(2,1)} %ow_ref.1, bf16[8,3072]{1,0:T(8,128)(2,1)} %bitcast.2, ...), custom_call_target="tpu_custom_call" | custom-call | tf_op jit(solution)/shard_map/pallas_call | solution.py:471
  64.0 1.5 %copy.12 = bf16[16,3072]{1,0:T(8,128)(2,1)} copy(bf16[16,3072]{1,0:T(8,128)(2,1)} %shard_map.100) | data formatting | bytes 196608

commit v3 on v2

--- a/solution.py
+++ b/solution.py
@@ -229,8 +229,8 @@
         def _():
             send_state(j, s).start()
 
-    up_tile = tile_of(up.shape[1], 384)
-    down_tile = tile_of(width_d, 512)
+    up_tile = tile_of(up.shape[1], 1152)
+    down_tile = tile_of(width_d, 1024)
 
     def expand(b):
         x = rows_buf[b, :, :width_d]

time: 65.7 us -> 65.3 us (level)
  no operation moved by 1% of the time
where the time goes in v3:
time: 65.3 us; the launch traced here: 65.2 us
  Pallas kernels  63.6 us (97%)
  local copies, waits for them, and re-layouts  1.54 us (2%)
    pallas_call x1, Pallas kernels, shards(): pl.pallas_call(functools.partial(layer, n, n_exp, cap), out_shape=jax.Sha...  63.6 us
    unnamed x1, local copies, waits for them, and re-layouts  1.54 us

profile of v3, /device:TPU:0, one launch (start us, length us, event | category | flops | bytes accessed | tf_op | source)
XLA Modules:
  0.0 65.2 jit_solution(16271925674587959263)
XLA Ops:
  0.0 63.6 %shard_map.100 = bf16[16,3072]{1,0:T(8,128)(2,1)} custom-call(bf16[128,256]{1,0:T(8,128)(2,1)} %q_ref.1, bf16[128,256]{1,0:T(8,128)(2,1)} %k_ref.1, bf16[128,256]{1,0:T(8,128)(2,1)} %v_ref.1, f32[2,128]{1,0:T(2,128)} %decay_ref.1, bf16[128,3072]{1,0:T(8,128)(2,1)} %res_ref.1, bf16[768,256]{1,0:T(8,128)(2,1)} %ow_ref.1, bf16[8,3072]{1,0:T(8,128)(2,1)} %bitcast.2, ...), custom_call_target="tpu_custom_call" | custom-call | tf_op jit(solution)/shard_map/pallas_call | solution.py:471
  63.6 1.5 %copy.12 = bf16[16,3072]{1,0:T(8,128)(2,1)} copy(bf16[16,3072]{1,0:T(8,128)(2,1)} %shard_map.100) | data formatting | bytes 196608
